TPU v7x, 512 devices: a whole 4x4x16 slice. The times are simulated.
512 devices in a mesh: sim: 32 (over z_lo, y, core), grp: 4 (over z_hi), gz: 4 (over x).
Axes of the slice: x: 4, y: 4, z: 16 (z_hi: 4, z_lo: 4; z = z_hi * 4 + z_lo), core: 2. Of those that a mesh axis runs over, the one named last changes fastest.
Arguments:
- fields: float32 [8, 2, 1024, 1024], P(None, None, 'sim', ('grp', 'gz')), may hold values from -6 to 6
- diffusivity: float32 [8], replicated, may hold values from 0.03 to 0.12
- velocity: float32 [2, 8], replicated, may hold values from -0.4 to 0.4
- coupling: float32 [8, 8], replicated, may hold values from -0.6 to 0.6
- basis_x: bfloat16 [1024, 128], replicated, may hold values from -0.1875 to 0.1875
- basis_y: bfloat16 [1024, 128], replicated, may hold values from -0.1875 to 0.1875
Outputs:
- fields_out: float32 [8, 2, 1024, 1024], P(None, None, 'sim', ('grp', 'gz'))
- gram_x: float32 [1024, 1024], P('sim', ('grp', 'gz'))
- gram_y: float32 [1024, 1024], P(('grp', 'gz'), 'sim')
- core: float32 [8, 2, 128, 128], P(None, None, 'sim', ('grp', 'gz'))
All inputs are finite; a program needn't handle non-finite values.
Results may differ from a plain program's by a relative error of at most 0.0003.
Values sent between devices are 32-bit elements; how exact they have to be, the bound alone decides.
A program may use at most 64 MiB of HBM per device.

v0:
```python
import jax
import jax.numpy as jnp
from jax import lax
from jax.sharding import PartitionSpec as P

NY = 1024
RANK = 128
STEPS = 2
time_step = 1.0
highest = lax.Precision.HIGHEST


def with_halo(cells, sides, width):
    for axis, dim in sides:
        count = lax.axis_size(axis)
        head = lax.slice_in_dim(cells, 0, width, axis=dim)
        tail = lax.slice_in_dim(cells, cells.shape[dim] - width, cells.shape[dim], axis=dim)
        cells = jnp.concatenate(
            [
                lax.ppermute(tail, axis, [(i, (i + 1) % count) for i in range(count)]),
                cells,
                lax.ppermute(head, axis, [((i + 1) % count, i) for i in range(count)]),
            ],
            axis=dim,
        )
    return cells


def rates(state, diffusivity, velocity, coupling):
    padded = with_halo(state, (("sim", 2), (("grp", "gz"), 3)), 1)
    center = padded[:, :, 1:-1, 1:-1]
    x_plus = padded[:, :, 2:, 1:-1]
    x_minus = padded[:, :, :-2, 1:-1]
    y_plus = padded[:, :, 1:-1, 2:]
    y_minus = padded[:, :, 1:-1, :-2]
    z_plus = jnp.roll(center, -1, 1)
    z_minus = jnp.roll(center, 1, 1)
    lapl = -6.0 * center + z_plus + z_minus + x_plus + x_minus + y_plus + y_minus
    grad_x = (x_plus - x_minus) * 0.5
    grad_y = (y_plus - y_minus) * 0.5
    react = jnp.einsum("fg,gzxy->fzxy", coupling, jnp.tanh(center), precision=highest)
    return (
        diffusivity[:, None, None, None] * lapl
        - velocity[0][:, None, None, None] * grad_x
        - velocity[1][:, None, None, None] * grad_y
        + react
    )


def shards(fields, diffusivity, velocity, coupling, basis_x, basis_y):
    state = fields
    for repeat in range(STEPS):
        first = rates(state, diffusivity, velocity, coupling)
        second = rates(state + 0.5 * time_step * first, diffusivity, velocity, coupling)
        third = rates(state + 0.5 * time_step * second, diffusivity, velocity, coupling)
        fourth = rates(state + time_step * third, diffusivity, velocity, coupling)
        state = state + time_step / 6.0 * (first + 2.0 * second + 2.0 * third + fourth)
    nfield = state.shape[0]
    depth = state.shape[1]
    x_rows = state.shape[2]
    y_cols = state.shape[3]
    basis_xf = basis_x.astype(jnp.float32)
    basis_yf = basis_y.astype(jnp.float32)
    block = jnp.einsum(
        "fzxy,fzwy->xw", state, lax.all_gather(state, "sim", axis=2, tiled=True), precision=highest
    )
    gram_rows = block
    own_basis = lax.dynamic_slice_in_dim(basis_xf, lax.axis_index("sim") * x_rows, x_rows, 0)
    partial_proj = jnp.einsum("xr,fzxy->fzry", own_basis, state, precision=highest)
    projected = lax.psum_scatter(partial_proj, "sim", scatter_dimension=2, tiled=True)
    gram_x = lax.psum_scatter(gram_rows, ("grp", "gz"), scatter_dimension=1, tiled=True) / (
        nfield * depth * NY
    )
    block = jnp.einsum(
        "fzry,fzrv->yv",
        projected,
        lax.all_gather(projected, ("grp", "gz"), axis=3, tiled=True),
        precision=highest,
    )
    own_basis_y = lax.dynamic_slice_in_dim(
        basis_yf, lax.axis_index(("grp", "gz")) * y_cols, y_cols, 0
    )
    partial_core = jnp.einsum("ys,fzry->fzrs", own_basis_y, projected, precision=highest)
    core = lax.psum_scatter(partial_core, ("grp", "gz"), scatter_dimension=3, tiled=True)
    gram_y = lax.psum_scatter(block, "sim", scatter_dimension=1, tiled=True) / (
        nfield * depth * RANK
    )
    return (state, gram_x, gram_y, core)


def solution(mesh):
    in_specs = (P(None, None, "sim", ("grp", "gz")), P(), P(), P(), P(), P())
    out_specs = (
        P(None, None, "sim", ("grp", "gz")),
        P("sim", ("grp", "gz")),
        P(("grp", "gz"), "sim"),
        P(None, None, "sim", ("grp", "gz")),
    )
    return jax.shard_map(shards, mesh=mesh, in_specs=in_specs, out_specs=out_specs, check_vma=False)
```

profile of v0, /device:TPU:8, one launch (start us, length us, event | category | flops | bytes accessed | tf_op | source)
XLA Modules:
  0.0 980.0 jit_solution(15464868327093606342)
XLA Ops:
  8.5 1.9 collective-permute-start.1
  10.4 3.6 collective-permute-start
  15.5 3.4 collective-permute-start.3
  18.9 13.5 %collective-permute-start.2 = (f32[8,2,34,1]{3,0,2,1:T(8,128)S(1)}, f32[8,2,34,1]{3,0,2,1:T(8,128)S(1)}, u32[]{:S(2)}, u32[]{:S(2)}) collective-permute-start(f32[8,2,34,1]{3,0,2,1:T(8,128)S(1)} %get-tuple-element.31), channel_id=1, source_target_pairs={{1,0},{2,1},{3,2},{4,3},{5,4},{6,5},{7,6},{8,7},{9,8},{10,9},{11,1... | collective-permute-start | bytes 6536 | tf_op jit(solution)/shard_map/ppermute | solution.py:22
  34.1 4.8 collective-permute-done.3
  39.0 15.9 %collective-permute-done.2 = f32[8,2,34,1]{3,0,2,1:T(8,128)S(1)} collective-permute-done((f32[8,2,34,1]{3,0,2,1:T(8,128)S(1)}, f32[8,2,34,1]{3,0,2,1:T(8,128)S(1)}, u32[]{:S(2)}, u32[]{:S(2)}) %collective-permute-start.2) | collective-permute-done | bytes 2208 | tf_op jit(solution)/shard_map/ppermute | solution.py:22
  54.9 1.6 multiply_add_fusion.3
  56.5 3.9 collective-permute-start.4
  60.4 1.9 collective-permute-start.5
  62.3 3.4 collective-permute-done.5
  65.9 1.9 collective-permute-start.7
  67.8 10.5 %collective-permute-start.6 = (f32[8,2,34,1]{3,0,2,1:T(8,128)S(1)}, f32[8,2,34,1]{3,0,2,1:T(8,128)S(1)}, u32[]{:S(2)}, u32[]{:S(2)}) collective-permute-start(f32[8,2,34,1]{3,0,2,1:T(8,128)S(1)} %get-tuple-element.29), channel_id=1, source_target_pairs={{1,0},{2,1},{3,2},{4,3},{5,4},{6,5},{7,6},{8,7},{9,8},{10,9},{11,1... | collective-permute-start | bytes 6536 | tf_op jit(solution)/shard_map/ppermute | solution.py:22
  78.4 9.8 collective-permute-done.7
  88.1 3.0 collective-permute-done.6
  91.1 1.5 multiply_add_fusion.2
  92.7 13.1 %collective-permute-start.8 = (f32[8,2,1,64]{3,0,2,1:T(8,128)S(1)}, f32[8,2,1,64]{3,0,2,1:T(8,128)S(1)}, u32[]{:S(2)}, u32[]{:S(2)}) collective-permute-start(f32[8,2,1,64]{3,0,2,1:T(8,128)S(1)} %get-tuple-element.53), channel_id=1, source_target_pairs={{16,0},{32,16},{48,32},{64,48},{80,64},{96,80},{112,96},{128,112},... | collective-permute-start | bytes 12296 | tf_op jit(solution)/shard_map/ppermute | solution.py:22
  105.8 1.9 collective-permute-start.9
  107.8 3.0 collective-permute-done.9
  110.9 1.9 collective-permute-start.11
  112.9 10.4 %collective-permute-start.10 = (f32[8,2,34,1]{3,0,2,1:T(8,128)S(1)}, f32[8,2,34,1]{3,0,2,1:T(8,128)S(1)}, u32[]{:S(2)}, u32[]{:S(2)}) collective-permute-start(f32[8,2,34,1]{3,0,2,1:T(8,128)S(1)} %get-tuple-element.27), channel_id=1, source_target_pairs={{1,0},{2,1},{3,2},{4,3},{5,4},{6,5},{7,6},{8,7},{9,8},{10,9},{11,1... | collective-permute-start | bytes 6536 | tf_op jit(solution)/shard_map/ppermute | solution.py:22
  123.3 17.0 %collective-permute-done.11 = f32[8,2,34,1]{3,0,2,1:T(8,128)S(1)} collective-permute-done((f32[8,2,34,1]{3,0,2,1:T(8,128)S(1)}, f32[8,2,34,1]{3,0,2,1:T(8,128)S(1)}, u32[]{:S(2)}, u32[]{:S(2)}) %collective-permute-start.11) | collective-permute-done | bytes 2208 | tf_op jit(solution)/shard_map/ppermute | solution.py:20
  140.9 1.9 collective-permute-start.12
  142.8 2.4 collective-permute-start.13
  145.2 2.5 collective-permute-done.13
  148.0 10.2 %collective-permute-start.14 = (f32[8,2,34,1]{3,0,2,1:T(8,128)S(1)}, f32[8,2,34,1]{3,0,2,1:T(8,128)S(1)}, u32[]{:S(2)}, u32[]{:S(2)}) collective-permute-start(f32[8,2,34,1]{3,0,2,1:T(8,128)S(1)} %get-tuple-element.25), channel_id=1, source_target_pairs={{1,0},{2,1},{3,2},{4,3},{5,4},{6,5},{7,6},{8,7},{9,8},{10,9},{11,1... | collective-permute-start | bytes 6536 | tf_op jit(solution)/shard_map/ppermute | solution.py:22
  158.2 1.9 collective-permute-start.15
  160.1 9.8 collective-permute-done.14
  169.9 16.0 %collective-permute-done.15 = f32[8,2,34,1]{3,0,2,1:T(8,128)S(1)} collective-permute-done((f32[8,2,34,1]{3,0,2,1:T(8,128)S(1)}, f32[8,2,34,1]{3,0,2,1:T(8,128)S(1)}, u32[]{:S(2)}, u32[]{:S(2)}) %collective-permute-start.15) | collective-permute-done | bytes 2208 | tf_op jit(solution)/shard_map/ppermute | solution.py:20
  186.5 1.9 collective-permute-start.16
  188.4 2.4 collective-permute-start.17
  190.9 2.5 collective-permute-done.17
  193.6 1.9 collective-permute-start.19
  195.5 9.9 %collective-permute-start.18 = (f32[8,2,34,1]{3,0,2,1:T(8,128)S(1)}, f32[8,2,34,1]{3,0,2,1:T(8,128)S(1)}, u32[]{:S(2)}, u32[]{:S(2)}) collective-permute-start(f32[8,2,34,1]{3,0,2,1:T(8,128)S(1)} %get-tuple-element.23), channel_id=1, source_target_pairs={{1,0},{2,1},{3,2},{4,3},{5,4},{6,5},{7,6},{8,7},{9,8},{10,9},{11,1... | collective-permute-start | bytes 6536 | tf_op jit(solution)/shard_map/ppermute | solution.py:22
  205.5 8.9 collective-permute-done.19
  214.8 1.9 collective-permute-start.20
  216.7 2.4 collective-permute-start.21
  219.1 2.5 collective-permute-done.21
  221.8 1.9 collective-permute-start.23
  223.8 9.9 %collective-permute-start.22 = (f32[8,2,34,1]{3,0,2,1:T(8,128)S(1)}, f32[8,2,34,1]{3,0,2,1:T(8,128)S(1)}, u32[]{:S(2)}, u32[]{:S(2)}) collective-permute-start(f32[8,2,34,1]{3,0,2,1:T(8,128)S(1)} %get-tuple-element.21), channel_id=1, source_target_pairs={{1,0},{2,1},{3,2},{4,3},{5,4},{6,5},{7,6},{8,7},{9,8},{10,9},{11,1... | collective-permute-start | bytes 6536 | tf_op jit(solution)/shard_map/ppermute | solution.py:22
  233.7 5.2 collective-permute-done.23
  238.9 1.2 collective-permute-done.22
  240.5 2.7 collective-permute-start.24
  243.3 1.9 collective-permute-start.25
  245.2 3.9 collective-permute-done.25
  249.3 1.9 collective-permute-start.27
  251.2 9.9 %collective-permute-start.26 = (f32[8,2,34,1]{3,0,2,1:T(8,128)S(1)}, f32[8,2,34,1]{3,0,2,1:T(8,128)S(1)}, u32[]{:S(2)}, u32[]{:S(2)}) collective-permute-start(f32[8,2,34,1]{3,0,2,1:T(8,128)S(1)} %get-tuple-element.19), channel_id=1, source_target_pairs={{1,0},{2,1},{3,2},{4,3},{5,4},{6,5},{7,6},{8,7},{9,8},{10,9},{11,1... | collective-permute-start | bytes 6536 | tf_op jit(solution)/shard_map/ppermute | solution.py:22
  261.2 8.2 collective-permute-done.27
  269.8 5.5 collective-permute-start.28
  275.3 1.9 collective-permute-start.29
  277.2 3.2 collective-permute-done.29
  280.6 7.2 collective-permute-start.30
  287.8 1.9 collective-permute-start.31
  289.8 10.9 %collective-permute-done.30 = f32[8,2,34,1]{3,0,2,1:T(8,128)S(1)} collective-permute-done((f32[8,2,34,1]{3,0,2,1:T(8,128)S(1)}, f32[8,2,34,1]{3,0,2,1:T(8,128)S(1)}, u32[]{:S(2)}, u32[]{:S(2)}) %collective-permute-start.30) | collective-permute-done | bytes 2208 | tf_op jit(solution)/shard_map/ppermute | solution.py:22
  300.7 5.3 collective-permute-done.31
  307.1 1.4 copy.67
  309.3 1.3 dynamic-slice
  311.3 181.6 %reduce-scatter.7.cloned.1.call-done = f32[8,2,4,64]{3,0,1,2:T(8,128)} async-done(((f32[8,2,128,64]{3,0,1,2:T(8,128)}), f32[8,2,4,64]{3,0,1,2:T(8,128)}) %reduce-scatter.7.cloned.1.call-update) | async-done | bytes 16400 | tf_op jit(solution)/shard_map/reduce_scatter | solution.py:70
  493.9 148.2 %all_gather.7 = f32[8,2,4,1024]{0,2,1,3:T(4,128)S(1)} all-gather(f32[8,2,4,64]{0,2,1,3:T(4,128)S(1)} %copy.68), channel_id=1, replica_groups=mesh['sim'=32,'grp'=4,'gz'=4] {'grp','gz'}, dimensions={3}, use_global_device_ids=true | all-gather | bytes 278528 | tf_op jit(solution)/shard_map/all_gather | solution.py:77
  642.1 7.6 fusion.4
  650.6 108.4 %all-reduce = f32[8,2,4,128]{3,0,2,1:T(8,128)S(1)} all-reduce(f32[8,2,4,128]{3,0,2,1:T(8,128)S(1)} %fusion.99), channel_id=5, replica_groups=mesh['sim'=32,'grp'=4,'gz'=4] {'grp','gz'}, use_global_device_ids=true, to_apply=%region_3.4.clone | all-reduce | flops 8192 | bytes 65536
  759.1 10.7 %fusion.7 = f32[1024,32]{1,0:T(8,128)} fusion(f32[8,2,32,64]{3,2,1,0:T(8,128)S(1)} %copy.71, f32[8,2,1024,64]{3,0,2,1:T(8,128)} %all-gather.2.cloned.1.call-done), kind=kOutput, calls=%fused_computation.5 | convolution fusion | flops 402653184 | bytes 4456448 | tf_op jit(solution)/shard_map/fzxy,fzwy->xw/dot_general | solution.py:64
  770.5 83.8 %reduce-scatter.9.cloned.1.call-done = f32[64,32]{0,1:T(8,128)} async-done(((f32[64,1024]{0,1:T(8,128)}), f32[64,32]{0,1:T(8,128)}) %reduce-scatter.9.cloned.1.call-update) | async-done | bytes 8208 | tf_op jit(solution)/shard_map/reduce_scatter | solution.py:85
  854.3 1.3 broadcast_multiply_fusion
  855.6 116.4 %reduce-scatter.11.cloned.1.call-done = f32[64,32]{1,0:T(8,128)} async-done(((f32[1024,32]{1,0:T(8,128)}), f32[64,32]{1,0:T(8,128)}) %reduce-scatter.11.cloned.1.call-update) | async-done | bytes 8208
  (86 shorter events, 14.2 us)
Async XLA Ops:
  7.2 299.3 %copy-start = (bf16[1024,128]{1,0:T(8,128)(2,1)S(1)}, bf16[1024,128]{1,0:T(8,128)(2,1)}, u32[]{:S(2)}) copy-start(bf16[1024,128]{1,0:T(8,128)(2,1)} %param.10) | copy-start | bytes 786436
  7.2 133.1 %copy-start.1 = (f32[8,2,32,64]{3,2,1,0:T(8,128)S(1)}, f32[8,2,32,64]{3,2,1,0:T(8,128)}, u32[]{:S(2)}) copy-start(f32[8,2,32,64]{3,2,1,0:T(8,128)} %param.6) | copy-start | bytes 393220
  7.2 133.1 %copy-start.5 = (f32[8,8]{1,0:T(8,128)S(1)}, f32[8,8]{1,0:T(8,128)}, u32[]{:S(2)}) copy-start(f32[8,8]{1,0:T(8,128)} %param.9) | copy-start | bytes 772
  7.2 133.1 %copy-start.6 = (f32[8]{0:T(128)S(1)}, f32[8]{0:T(128)}, u32[]{:S(2)}) copy-start(f32[8]{0:T(128)} %param.7) | copy-start | bytes 100
  7.2 485.7 %reduce-scatter.7.cloned.1.call-start = ((), (), s32[]{:S(2)}) async-start(), calls=%async_computation.4 | async-start | bytes 1081344 | tf_op jit(solution)/shard_map/reduce_scatter | solution.py:70
  8.5 5.6 collective-permute-start.1
  10.4 5.0 collective-permute-start
  15.5 23.4 %collective-permute-start.3 = (f32[8,2,34,1]{3,0,2,1:T(8,128)S(1)}, f32[8,2,34,1]{3,0,2,1:T(8,128)S(1)}, u32[]{:S(2)}, u32[]{:S(2)}) collective-permute-start(f32[8,2,34,1]{3,0,2,1:T(8,128)S(1)} %get-tuple-element.30), channel_id=1, source_target_pairs={{0,1},{1,2},{2,3},{3,4},{4,5},{5,6},{6,7},{7,8},{8,9},{9,10},{10,1... | collective-permute-start | bytes 6536 | tf_op jit(solution)/shard_map/ppermute | solution.py:20
  18.9 36.0 %collective-permute-start.2 = (f32[8,2,34,1]{3,0,2,1:T(8,128)S(1)}, f32[8,2,34,1]{3,0,2,1:T(8,128)S(1)}, u32[]{:S(2)}, u32[]{:S(2)}) collective-permute-start(f32[8,2,34,1]{3,0,2,1:T(8,128)S(1)} %get-tuple-element.31), channel_id=1, source_target_pairs={{1,0},{2,1},{3,2},{4,3},{5,4},{6,5},{7,6},{8,7},{9,8},{10,9},{11,1... | collective-permute-start | bytes 6536 | tf_op jit(solution)/shard_map/ppermute | solution.py:22
  56.5 5.8 collective-permute-start.4
  60.4 5.3 collective-permute-start.5
  65.9 22.2 %collective-permute-start.7 = (f32[8,2,34,1]{3,0,2,1:T(8,128)S(1)}, f32[8,2,34,1]{3,0,2,1:T(8,128)S(1)}, u32[]{:S(2)}, u32[]{:S(2)}) collective-permute-start(f32[8,2,34,1]{3,0,2,1:T(8,128)S(1)} %get-tuple-element.28), channel_id=1, source_target_pairs={{0,1},{1,2},{2,3},{3,4},{4,5},{5,6},{6,7},{7,8},{8,9},{9,10},{10,1... | collective-permute-start | bytes 6536 | tf_op jit(solution)/shard_map/ppermute | solution.py:20
  67.8 23.3 %collective-permute-start.6 = (f32[8,2,34,1]{3,0,2,1:T(8,128)S(1)}, f32[8,2,34,1]{3,0,2,1:T(8,128)S(1)}, u32[]{:S(2)}, u32[]{:S(2)}) collective-permute-start(f32[8,2,34,1]{3,0,2,1:T(8,128)S(1)} %get-tuple-element.29), channel_id=1, source_target_pairs={{1,0},{2,1},{3,2},{4,3},{5,4},{6,5},{7,6},{8,7},{9,8},{10,9},{11,1... | collective-permute-start | bytes 6536 | tf_op jit(solution)/shard_map/ppermute | solution.py:22
  92.7 15.1 %collective-permute-start.8 = (f32[8,2,1,64]{3,0,2,1:T(8,128)S(1)}, f32[8,2,1,64]{3,0,2,1:T(8,128)S(1)}, u32[]{:S(2)}, u32[]{:S(2)}) collective-permute-start(f32[8,2,1,64]{3,0,2,1:T(8,128)S(1)} %get-tuple-element.53), channel_id=1, source_target_pairs={{16,0},{32,16},{48,32},{64,48},{80,64},{96,80},{112,96},{128,112},... | collective-permute-start | bytes 12296 | tf_op jit(solution)/shard_map/ppermute | solution.py:22
  105.8 5.0 collective-permute-start.9
  110.9 29.4 %collective-permute-start.11 = (f32[8,2,34,1]{3,0,2,1:T(8,128)S(1)}, f32[8,2,34,1]{3,0,2,1:T(8,128)S(1)}, u32[]{:S(2)}, u32[]{:S(2)}) collective-permute-start(f32[8,2,34,1]{3,0,2,1:T(8,128)S(1)} %get-tuple-element.26), channel_id=1, source_target_pairs={{0,1},{1,2},{2,3},{3,4},{4,5},{5,6},{6,7},{7,8},{8,9},{9,10},{10,1... | collective-permute-start | bytes 6536 | tf_op jit(solution)/shard_map/ppermute | solution.py:20
  112.9 27.4 %collective-permute-start.10 = (f32[8,2,34,1]{3,0,2,1:T(8,128)S(1)}, f32[8,2,34,1]{3,0,2,1:T(8,128)S(1)}, u32[]{:S(2)}, u32[]{:S(2)}) collective-permute-start(f32[8,2,34,1]{3,0,2,1:T(8,128)S(1)} %get-tuple-element.27), channel_id=1, source_target_pairs={{1,0},{2,1},{3,2},{4,3},{5,4},{6,5},{7,6},{8,7},{9,8},{10,9},{11,1... | collective-permute-start | bytes 6536 | tf_op jit(solution)/shard_map/ppermute | solution.py:22
  140.9 4.3 collective-permute-start.12
  142.8 5.0 collective-permute-start.13
  148.0 21.9 %collective-permute-start.14 = (f32[8,2,34,1]{3,0,2,1:T(8,128)S(1)}, f32[8,2,34,1]{3,0,2,1:T(8,128)S(1)}, u32[]{:S(2)}, u32[]{:S(2)}) collective-permute-start(f32[8,2,34,1]{3,0,2,1:T(8,128)S(1)} %get-tuple-element.25), channel_id=1, source_target_pairs={{1,0},{2,1},{3,2},{4,3},{5,4},{6,5},{7,6},{8,7},{9,8},{10,9},{11,1... | collective-permute-start | bytes 6536 | tf_op jit(solution)/shard_map/ppermute | solution.py:22
  158.2 27.7 %collective-permute-start.15 = (f32[8,2,34,1]{3,0,2,1:T(8,128)S(1)}, f32[8,2,34,1]{3,0,2,1:T(8,128)S(1)}, u32[]{:S(2)}, u32[]{:S(2)}) collective-permute-start(f32[8,2,34,1]{3,0,2,1:T(8,128)S(1)} %get-tuple-element.24), channel_id=1, source_target_pairs={{0,1},{1,2},{2,3},{3,4},{4,5},{5,6},{6,7},{7,8},{8,9},{9,10},{10,1... | collective-permute-start | bytes 6536 | tf_op jit(solution)/shard_map/ppermute | solution.py:20
  186.5 4.3 collective-permute-start.16
  188.4 5.0 collective-permute-start.17
  193.6 20.8 %collective-permute-start.19 = (f32[8,2,34,1]{3,0,2,1:T(8,128)S(1)}, f32[8,2,34,1]{3,0,2,1:T(8,128)S(1)}, u32[]{:S(2)}, u32[]{:S(2)}) collective-permute-start(f32[8,2,34,1]{3,0,2,1:T(8,128)S(1)} %get-tuple-element.22), channel_id=1, source_target_pairs={{0,1},{1,2},{2,3},{3,4},{4,5},{5,6},{6,7},{7,8},{8,9},{9,10},{10,1... | collective-permute-start | bytes 6536 | tf_op jit(solution)/shard_map/ppermute | solution.py:20
  195.5 18.8 %collective-permute-start.18 = (f32[8,2,34,1]{3,0,2,1:T(8,128)S(1)}, f32[8,2,34,1]{3,0,2,1:T(8,128)S(1)}, u32[]{:S(2)}, u32[]{:S(2)}) collective-permute-start(f32[8,2,34,1]{3,0,2,1:T(8,128)S(1)} %get-tuple-element.23), channel_id=1, source_target_pairs={{1,0},{2,1},{3,2},{4,3},{5,4},{6,5},{7,6},{8,7},{9,8},{10,9},{11,1... | collective-permute-start | bytes 6536 | tf_op jit(solution)/shard_map/ppermute | solution.py:22
  214.8 4.3 collective-permute-start.20
  216.7 5.0 collective-permute-start.21
  221.8 17.1 %collective-permute-start.23 = (f32[8,2,34,1]{3,0,2,1:T(8,128)S(1)}, f32[8,2,34,1]{3,0,2,1:T(8,128)S(1)}, u32[]{:S(2)}, u32[]{:S(2)}) collective-permute-start(f32[8,2,34,1]{3,0,2,1:T(8,128)S(1)} %get-tuple-element.20), channel_id=1, source_target_pairs={{0,1},{1,2},{2,3},{3,4},{4,5},{5,6},{6,7},{7,8},{8,9},{9,10},{10,1... | collective-permute-start | bytes 6536 | tf_op jit(solution)/shard_map/ppermute | solution.py:20
  223.8 16.3 %collective-permute-start.22 = (f32[8,2,34,1]{3,0,2,1:T(8,128)S(1)}, f32[8,2,34,1]{3,0,2,1:T(8,128)S(1)}, u32[]{:S(2)}, u32[]{:S(2)}) collective-permute-start(f32[8,2,34,1]{3,0,2,1:T(8,128)S(1)} %get-tuple-element.21), channel_id=1, source_target_pairs={{1,0},{2,1},{3,2},{4,3},{5,4},{6,5},{7,6},{8,7},{9,8},{10,9},{11,1... | collective-permute-start | bytes 6536 | tf_op jit(solution)/shard_map/ppermute | solution.py:22
  240.5 4.7 collective-permute-start.24
  243.3 5.8 collective-permute-start.25
  249.3 20.1 %collective-permute-start.27 = (f32[8,2,34,1]{3,0,2,1:T(8,128)S(1)}, f32[8,2,34,1]{3,0,2,1:T(8,128)S(1)}, u32[]{:S(2)}, u32[]{:S(2)}) collective-permute-start(f32[8,2,34,1]{3,0,2,1:T(8,128)S(1)} %get-tuple-element.18), channel_id=1, source_target_pairs={{0,1},{1,2},{2,3},{3,4},{4,5},{5,6},{6,7},{7,8},{8,9},{9,10},{10,1... | collective-permute-start | bytes 6536 | tf_op jit(solution)/shard_map/ppermute | solution.py:20
  251.2 18.2 %collective-permute-start.26 = (f32[8,2,34,1]{3,0,2,1:T(8,128)S(1)}, f32[8,2,34,1]{3,0,2,1:T(8,128)S(1)}, u32[]{:S(2)}, u32[]{:S(2)}) collective-permute-start(f32[8,2,34,1]{3,0,2,1:T(8,128)S(1)} %get-tuple-element.19), channel_id=1, source_target_pairs={{1,0},{2,1},{3,2},{4,3},{5,4},{6,5},{7,6},{8,7},{9,8},{10,9},{11,1... | collective-permute-start | bytes 6536 | tf_op jit(solution)/shard_map/ppermute | solution.py:22
  269.8 7.4 collective-permute-start.28
  275.3 5.2 collective-permute-start.29
  280.6 20.0 %collective-permute-start.30 = (f32[8,2,34,1]{3,0,2,1:T(8,128)S(1)}, f32[8,2,34,1]{3,0,2,1:T(8,128)S(1)}, u32[]{:S(2)}, u32[]{:S(2)}) collective-permute-start(f32[8,2,34,1]{3,0,2,1:T(8,128)S(1)} %get-tuple-element.17), channel_id=1, source_target_pairs={{1,0},{2,1},{3,2},{4,3},{5,4},{6,5},{7,6},{8,7},{9,8},{10,9},{11,1... | collective-permute-start | bytes 6536 | tf_op jit(solution)/shard_map/ppermute | solution.py:22
  287.8 18.1 %collective-permute-start.31 = (f32[8,2,34,1]{3,0,2,1:T(8,128)S(1)}, f32[8,2,34,1]{3,0,2,1:T(8,128)S(1)}, u32[]{:S(2)}, u32[]{:S(2)}) collective-permute-start(f32[8,2,34,1]{3,0,2,1:T(8,128)S(1)} %get-tuple-element.16), channel_id=1, source_target_pairs={{0,1},{1,2},{2,3},{3,4},{4,5},{5,6},{6,7},{7,8},{8,9},{9,10},{10,1... | collective-permute-start | bytes 6536 | tf_op jit(solution)/shard_map/ppermute | solution.py:20
  306.4 2.2 copy-start.3
  306.5 463.3 %copy-start.2 = (f32[8,2,32,64]{3,2,1,0:T(8,128)}, f32[8,2,32,64]{3,2,1,0:T(8,128)S(1)}, u32[]{:S(2)}) copy-start(f32[8,2,32,64]{3,2,1,0:T(8,128)S(1)} %copy.71) | copy-start | bytes 393220
  308.5 450.5 %all-gather.2.cloned.1.call-start = ((), (), s32[]{:S(2)}) async-start(), calls=%async_computation.3 | async-start | bytes 8650752 | tf_op jit(solution)/shard_map/all_gather | solution.py:65
  309.3 545.0 %reduce-scatter.9.cloned.1.call-start = ((), (), s32[]{:S(2)}) async-start(), calls=%async_computation.5 | async-start | bytes 540672 | tf_op jit(solution)/shard_map/reduce_scatter | solution.py:85
  492.9 156.9 %copy-start.4 = (f32[8,2,4,64]{3,0,1,2:T(8,128)S(1)}, f32[8,2,4,64]{3,0,1,2:T(8,128)}, u32[]{:S(2)}) copy-start(f32[8,2,4,64]{3,0,1,2:T(8,128)} %reduce-scatter.7.cloned.1.call-done) | copy-start | bytes 49156
  649.7 322.3 %reduce-scatter.11.cloned.1.call-start = ((), (), s32[]{:S(2)}) async-start(), calls=%async_computation.6 | async-start | bytes 557056
Sparse Core Ops, SparseCore 0:
  308.6 184.2 reduce-scatter.6
  495.3 193.5 all-gather.1
  691.9 162.3 reduce-scatter.8
  858.2 113.7 reduce-scatter.10
where the time goes:
time: 981 us; the launch traced here: 980 us
  waiting for transfers between devices  520 us (53%)
  blocking collectives  257 us (26%)
  starting transfers between devices  150 us (15%)
  matrix products  25.9 us (3%)
  between operations  15.2 us (2%)
    reduce_scatter x1, waiting for transfers between devices, shards(): lax.psum_scatter(partial_proj, 'sim', scatter_dimension=2, tiled=True)  182 us
    all_gather x1, blocking collectives, shards(): lax.all_gather(projected, ('grp', 'gz'), axis=3, tiled=True)  148 us
    unnamed x5, waiting for transfers between devices  117 us
    ppermute x16, starting transfers between devices, with_halo(): lax.ppermute(head, axis, [((i + 1) % count, i) for i in range(count)])  116 us
    unnamed x1, blocking collectives  108 us
    ppermute x16, waiting for transfers between devices, with_halo(): lax.ppermute(tail, axis, [(i, (i + 1) % count) for i in range(count)])  96.2 us
    reduce_scatter x1, waiting for transfers between devices, shards(): lax.psum_scatter(block, 'sim', scatter_dimension=1, tiled=True)  83.8 us
    ppermute x16, waiting for transfers between devices, with_halo(): lax.ppermute(head, axis, [((i + 1) % count, i) for i in range(count)])  41 us
  transfers between devices with their start and end apart: 36, of which 24 were waited for; matrix products, arithmetic and copies ran while one was open for 3% of the time, Pallas kernels for 0%

commit v1 on v0

--- a/solution.py
+++ b/solution.py
@@ -74,7 +74,12 @@
     block = jnp.einsum(
         "fzry,fzrv->yv",
         projected,
-        lax.all_gather(projected, ("grp", "gz"), axis=3, tiled=True),
+        jnp.concatenate(
+            lax.all_to_all(
+                jnp.stack([projected] * lax.axis_size(("grp", "gz"))), ("grp", "gz"), 0, 0
+            ),
+            axis=3,
+        ),
         precision=highest,
     )
     own_basis_y = lax.dynamic_slice_in_dim(

time: 981 us -> 842 us (0.86)
  blocking collectives: 257 us -> 92.8 us
  starting transfers between devices: 150 us -> 164 us
  waiting for transfers between devices: 520 us -> 532 us
    all_gather x1 -> x0, blocking collectives: 148 us -> none  [shards(): lax.all_gather(projected, ('grp', 'gz'), axis=3, tiled=True)]
    unnamed x1, blocking collectives: 108 us -> 92.8 us
    all_to_all x0 -> x1, waiting for transfers between devices: none -> 13.9 us  [shards(): lax.all_to_all(jnp.stack([projected] * lax.axis_size(('grp', 'gz'))), ('g...]
    all_to_all x0 -> x1, starting transfers between devices: none -> 13.4 us  [shards(): lax.all_to_all(jnp.stack([projected] * lax.axis_size(('grp', 'gz'))), ('g...]
  transfers between devices with their start and end apart: 36 -> 37, of which waited for: 24 -> 25; matrix products, arithmetic and copies ran while one was open for 3% -> 3% of each run, Pallas kernels for 0% -> 0%
where the time goes in v1:
time: 842 us; the launch traced here: 840 us
  waiting for transfers between devices  532 us (63%)
  starting transfers between devices  164 us (19%)
  blocking collectives  92.8 us (11%)
  matrix products  20.8 us (2%)
  between operations  15.2 us (2%)
  local copies, waits for them, and re-layouts  11.8 us (1%)
    reduce_scatter x1, waiting for transfers between devices, shards(): lax.psum_scatter(partial_proj, 'sim', scatter_dimension=2, tiled=True)  179 us
    unnamed x5, waiting for transfers between devices  117 us
    ppermute x16, starting transfers between devices, with_halo(): lax.ppermute(head, axis, [((i + 1) % count, i) for i in range(count)])  116 us
    ppermute x16, waiting for transfers between devices, with_halo(): lax.ppermute(tail, axis, [(i, (i + 1) % count) for i in range(count)])  96.2 us
    unnamed x1, blocking collectives  92.8 us
    reduce_scatter x1, waiting for transfers between devices, shards(): lax.psum_scatter(block, 'sim', scatter_dimension=1, tiled=True)  84.7 us
    ppermute x16, waiting for transfers between devices, with_halo(): lax.ppermute(head, axis, [((i + 1) % count, i) for i in range(count)])  41 us
    ppermute x16, starting transfers between devices, with_halo(): lax.ppermute(tail, axis, [(i, (i + 1) % count) for i in range(count)])  33.7 us
  transfers between devices with their start and end apart: 37, of which 25 were waited for; matrix products, arithmetic and copies ran while one was open for 3% of the time, Pallas kernels for 0%

profile of v1, /device:TPU:8, one launch (start us, length us, event | category | flops | bytes accessed | tf_op | source)
XLA Modules:
  0.0 840.1 jit_solution(13027976921097842774)
XLA Ops:
  8.5 1.9 collective-permute-start.1
  10.4 3.6 collective-permute-start
  15.5 3.4 collective-permute-start.3
  18.9 13.5 %collective-permute-start.2 = (f32[8,2,34,1]{3,0,2,1:T(8,128)S(1)}, f32[8,2,34,1]{3,0,2,1:T(8,128)S(1)}, u32[]{:S(2)}, u32[]{:S(2)}) collective-permute-start(f32[8,2,34,1]{3,0,2,1:T(8,128)S(1)} %get-tuple-element.27), channel_id=1, source_target_pairs={{1,0},{2,1},{3,2},{4,3},{5,4},{6,5},{7,6},{8,7},{9,8},{10,9},{11,1... | collective-permute-start | bytes 6536 | tf_op jit(solution)/shard_map/ppermute | solution.py:22
  34.1 4.8 collective-permute-done.3
  39.0 15.9 %collective-permute-done.2 = f32[8,2,34,1]{3,0,2,1:T(8,128)S(1)} collective-permute-done((f32[8,2,34,1]{3,0,2,1:T(8,128)S(1)}, f32[8,2,34,1]{3,0,2,1:T(8,128)S(1)}, u32[]{:S(2)}, u32[]{:S(2)}) %collective-permute-start.2) | collective-permute-done | bytes 2208 | tf_op jit(solution)/shard_map/ppermute | solution.py:22
  54.9 1.6 multiply_add_fusion.3
  56.5 3.9 collective-permute-start.4
  60.4 1.9 collective-permute-start.5
  62.3 3.4 collective-permute-done.5
  65.9 1.9 collective-permute-start.7
  67.8 10.5 %collective-permute-start.6 = (f32[8,2,34,1]{3,0,2,1:T(8,128)S(1)}, f32[8,2,34,1]{3,0,2,1:T(8,128)S(1)}, u32[]{:S(2)}, u32[]{:S(2)}) collective-permute-start(f32[8,2,34,1]{3,0,2,1:T(8,128)S(1)} %get-tuple-element.25), channel_id=1, source_target_pairs={{1,0},{2,1},{3,2},{4,3},{5,4},{6,5},{7,6},{8,7},{9,8},{10,9},{11,1... | collective-permute-start | bytes 6536 | tf_op jit(solution)/shard_map/ppermute | solution.py:22
  78.4 9.8 %collective-permute-done.7 = f32[8,2,34,1]{3,0,2,1:T(8,128)S(1)} collective-permute-done((f32[8,2,34,1]{3,0,2,1:T(8,128)S(1)}, f32[8,2,34,1]{3,0,2,1:T(8,128)S(1)}, u32[]{:S(2)}, u32[]{:S(2)}) %collective-permute-start.7) | collective-permute-done | bytes 2208 | tf_op jit(solution)/shard_map/ppermute | solution.py:20
  88.1 3.0 collective-permute-done.6
  91.1 1.5 multiply_add_fusion.2
  92.7 13.1 %collective-permute-start.8 = (f32[8,2,1,64]{3,0,2,1:T(8,128)S(1)}, f32[8,2,1,64]{3,0,2,1:T(8,128)S(1)}, u32[]{:S(2)}, u32[]{:S(2)}) collective-permute-start(f32[8,2,1,64]{3,0,2,1:T(8,128)S(1)} %get-tuple-element.49), channel_id=1, source_target_pairs={{16,0},{32,16},{48,32},{64,48},{80,64},{96,80},{112,96},{128,112},... | collective-permute-start | bytes 12296 | tf_op jit(solution)/shard_map/ppermute | solution.py:22
  105.8 1.9 collective-permute-start.9
  107.8 3.0 collective-permute-done.9
  110.9 1.9 collective-permute-start.11
  112.9 10.4 %collective-permute-start.10 = (f32[8,2,34,1]{3,0,2,1:T(8,128)S(1)}, f32[8,2,34,1]{3,0,2,1:T(8,128)S(1)}, u32[]{:S(2)}, u32[]{:S(2)}) collective-permute-start(f32[8,2,34,1]{3,0,2,1:T(8,128)S(1)} %get-tuple-element.23), channel_id=1, source_target_pairs={{1,0},{2,1},{3,2},{4,3},{5,4},{6,5},{7,6},{8,7},{9,8},{10,9},{11,1... | collective-permute-start | bytes 6536 | tf_op jit(solution)/shard_map/ppermute | solution.py:22
  123.3 17.0 %collective-permute-done.11 = f32[8,2,34,1]{3,0,2,1:T(8,128)S(1)} collective-permute-done((f32[8,2,34,1]{3,0,2,1:T(8,128)S(1)}, f32[8,2,34,1]{3,0,2,1:T(8,128)S(1)}, u32[]{:S(2)}, u32[]{:S(2)}) %collective-permute-start.11) | collective-permute-done | bytes 2208 | tf_op jit(solution)/shard_map/ppermute | solution.py:20
  140.9 1.9 collective-permute-start.12
  142.8 2.4 collective-permute-start.13
  145.2 2.5 collective-permute-done.13
  148.0 10.2 %collective-permute-start.14 = (f32[8,2,34,1]{3,0,2,1:T(8,128)S(1)}, f32[8,2,34,1]{3,0,2,1:T(8,128)S(1)}, u32[]{:S(2)}, u32[]{:S(2)}) collective-permute-start(f32[8,2,34,1]{3,0,2,1:T(8,128)S(1)} %get-tuple-element.21), channel_id=1, source_target_pairs={{1,0},{2,1},{3,2},{4,3},{5,4},{6,5},{7,6},{8,7},{9,8},{10,9},{11,1... | collective-permute-start | bytes 6536 | tf_op jit(solution)/shard_map/ppermute | solution.py:22
  158.2 1.9 collective-permute-start.15
  160.1 9.8 %collective-permute-done.14 = f32[8,2,34,1]{3,0,2,1:T(8,128)S(1)} collective-permute-done((f32[8,2,34,1]{3,0,2,1:T(8,128)S(1)}, f32[8,2,34,1]{3,0,2,1:T(8,128)S(1)}, u32[]{:S(2)}, u32[]{:S(2)}) %collective-permute-start.14) | collective-permute-done | bytes 2208 | tf_op jit(solution)/shard_map/ppermute | solution.py:22
  169.9 16.0 %collective-permute-done.15 = f32[8,2,34,1]{3,0,2,1:T(8,128)S(1)} collective-permute-done((f32[8,2,34,1]{3,0,2,1:T(8,128)S(1)}, f32[8,2,34,1]{3,0,2,1:T(8,128)S(1)}, u32[]{:S(2)}, u32[]{:S(2)}) %collective-permute-start.15) | collective-permute-done | bytes 2208 | tf_op jit(solution)/shard_map/ppermute | solution.py:20
  186.5 1.9 collective-permute-start.16
  188.4 2.4 collective-permute-start.17
  190.9 2.5 collective-permute-done.17
  193.6 1.9 collective-permute-start.19
  195.5 9.9 %collective-permute-start.18 = (f32[8,2,34,1]{3,0,2,1:T(8,128)S(1)}, f32[8,2,34,1]{3,0,2,1:T(8,128)S(1)}, u32[]{:S(2)}, u32[]{:S(2)}) collective-permute-start(f32[8,2,34,1]{3,0,2,1:T(8,128)S(1)} %get-tuple-element.19), channel_id=1, source_target_pairs={{1,0},{2,1},{3,2},{4,3},{5,4},{6,5},{7,6},{8,7},{9,8},{10,9},{11,1... | collective-permute-start | bytes 6536 | tf_op jit(solution)/shard_map/ppermute | solution.py:22
  205.5 8.9 %collective-permute-done.19 = f32[8,2,34,1]{3,0,2,1:T(8,128)S(1)} collective-permute-done((f32[8,2,34,1]{3,0,2,1:T(8,128)S(1)}, f32[8,2,34,1]{3,0,2,1:T(8,128)S(1)}, u32[]{:S(2)}, u32[]{:S(2)}) %collective-permute-start.19) | collective-permute-done | bytes 2208 | tf_op jit(solution)/shard_map/ppermute | solution.py:20
  214.8 1.9 collective-permute-start.20
  216.7 2.4 collective-permute-start.21
  219.1 2.5 collective-permute-done.21
  221.8 1.9 collective-permute-start.23
  223.8 9.9 %collective-permute-start.22 = (f32[8,2,34,1]{3,0,2,1:T(8,128)S(1)}, f32[8,2,34,1]{3,0,2,1:T(8,128)S(1)}, u32[]{:S(2)}, u32[]{:S(2)}) collective-permute-start(f32[8,2,34,1]{3,0,2,1:T(8,128)S(1)} %get-tuple-element.17), channel_id=1, source_target_pairs={{1,0},{2,1},{3,2},{4,3},{5,4},{6,5},{7,6},{8,7},{9,8},{10,9},{11,1... | collective-permute-start | bytes 6536 | tf_op jit(solution)/shard_map/ppermute | solution.py:22
  233.7 5.2 collective-permute-done.23
  240.5 2.7 collective-permute-start.24
  243.3 1.9 collective-permute-start.25
  245.2 3.9 collective-permute-done.25
  249.3 1.9 collective-permute-start.27
  251.2 9.9 %collective-permute-start.26 = (f32[8,2,34,1]{3,0,2,1:T(8,128)S(1)}, f32[8,2,34,1]{3,0,2,1:T(8,128)S(1)}, u32[]{:S(2)}, u32[]{:S(2)}) collective-permute-start(f32[8,2,34,1]{3,0,2,1:T(8,128)S(1)} %get-tuple-element.15), channel_id=1, source_target_pairs={{1,0},{2,1},{3,2},{4,3},{5,4},{6,5},{7,6},{8,7},{9,8},{10,9},{11,1... | collective-permute-start | bytes 6536 | tf_op jit(solution)/shard_map/ppermute | solution.py:22
  261.2 8.2 collective-permute-done.27
  269.8 5.5 collective-permute-start.28
  275.3 1.9 collective-permute-start.29
  277.2 3.2 collective-permute-done.29
  280.6 7.2 collective-permute-start.30
  287.8 1.9 collective-permute-start.31
  289.8 10.9 %collective-permute-done.30 = f32[8,2,34,1]{3,0,2,1:T(8,128)S(1)} collective-permute-done((f32[8,2,34,1]{3,0,2,1:T(8,128)S(1)}, f32[8,2,34,1]{3,0,2,1:T(8,128)S(1)}, u32[]{:S(2)}, u32[]{:S(2)}) %collective-permute-start.30) | collective-permute-done | bytes 2208 | tf_op jit(solution)/shard_map/ppermute | solution.py:22
  300.7 5.3 collective-permute-done.31
  307.1 1.4 copy.47
  309.3 178.6 %reduce-scatter.7.cloned.1.call-done = f32[8,2,4,64]{3,0,1,2:T(8,128)} async-done(((f32[8,2,128,64]{3,0,1,2:T(8,128)}), f32[8,2,4,64]{3,0,1,2:T(8,128)}) %reduce-scatter.7.cloned.1.call-update) | async-done | bytes 16400 | tf_op jit(solution)/shard_map/reduce_scatter | solution.py:70
  489.7 13.4 %all-to-all-start = ((f32[16,1,4096]{2,1,0:T(1,128)}), f32[16,1,4096]{2,1,0:T(1,128)S(1)}, u32[]{:S(2)}, u32[]{:S(2)}) async-start(f32[16,1,4096]{2,1,0:T(1,128)} %reshape.35), calls=%async_computation.1 | async-start | bytes 524288 | tf_op jit(solution)/shard_map/all_to_all | solution.py:78
  503.4 1.3 dynamic-slice
  505.3 13.9 %all-to-all-done = f32[16,1,4096]{2,1,0:T(1,128)S(1)} async-done(((f32[16,1,4096]{2,1,0:T(1,128)}), f32[16,1,4096]{2,1,0:T(1,128)S(1)}, u32[]{:S(2)}, u32[]{:S(2)}) %all-to-all-start) | async-done | bytes 262176 | tf_op jit(solution)/shard_map/all_to_all | solution.py:78
  521.7 2.5 convolution_bitcast_fusion
  525.2 92.8 %all-reduce = f32[8,2,4,128]{3,0,2,1:T(8,128)S(1)} all-reduce(f32[8,2,4,128]{3,0,2,1:T(8,128)S(1)} %fusion.94), channel_id=5, replica_groups=mesh['sim'=32,'grp'=4,'gz'=4] {'grp','gz'}, use_global_device_ids=true, to_apply=%region_3.4.clone | all-reduce | flops 8192 | bytes 65536
  618.0 10.7 %fusion.2 = f32[1024,32]{1,0:T(8,128)} fusion(f32[8,2,32,64]{3,2,1,0:T(8,128)S(1)} %copy.50, f32[8,2,1024,64]{3,0,2,1:T(8,128)} %all-gather.2.cloned.1.call-done), kind=kOutput, calls=%fused_computation.2 | convolution fusion | flops 402653184 | bytes 4456448 | tf_op jit(solution)/shard_map/fzxy,fzwy->xw/dot_general | solution.py:64
  629.5 84.7 %reduce-scatter.9.cloned.1.call-done = f32[64,32]{0,1:T(8,128)} async-done(((f32[64,1024]{0,1:T(8,128)}), f32[64,32]{0,1:T(8,128)}) %reduce-scatter.9.cloned.1.call-update) | async-done | bytes 8208 | tf_op jit(solution)/shard_map/reduce_scatter | solution.py:90
  714.2 1.3 broadcast_multiply_fusion
  715.5 116.6 %reduce-scatter.11.cloned.1.call-done = f32[64,32]{1,0:T(8,128)} async-done(((f32[1024,32]{1,0:T(8,128)}), f32[64,32]{1,0:T(8,128)}) %reduce-scatter.11.cloned.1.call-update) | async-done | bytes 8208
  (92 shorter events, 18.9 us)
Async XLA Ops:
  7.2 299.3 %copy-start = (bf16[1024,128]{1,0:T(8,128)(2,1)S(1)}, bf16[1024,128]{1,0:T(8,128)(2,1)}, u32[]{:S(2)}) copy-start(bf16[1024,128]{1,0:T(8,128)(2,1)} %param.10) | copy-start | bytes 786436
  7.2 133.1 %copy-start.1 = (f32[8,2,32,64]{3,2,1,0:T(8,128)S(1)}, f32[8,2,32,64]{3,2,1,0:T(8,128)}, u32[]{:S(2)}) copy-start(f32[8,2,32,64]{3,2,1,0:T(8,128)} %param.6) | copy-start | bytes 393220
  7.2 133.1 %copy-start.4 = (f32[8,8]{1,0:T(8,128)S(1)}, f32[8,8]{1,0:T(8,128)}, u32[]{:S(2)}) copy-start(f32[8,8]{1,0:T(8,128)} %param.9) | copy-start | bytes 772
  7.2 133.1 %copy-start.5 = (f32[8]{0:T(128)S(1)}, f32[8]{0:T(128)}, u32[]{:S(2)}) copy-start(f32[8]{0:T(128)} %param.7) | copy-start | bytes 100
  7.2 480.7 %reduce-scatter.7.cloned.1.call-start = ((), (), s32[]{:S(2)}) async-start(), calls=%async_computation.5 | async-start | bytes 1081344 | tf_op jit(solution)/shard_map/reduce_scatter | solution.py:70
  8.5 5.6 collective-permute-start.1
  10.4 5.0 collective-permute-start
  15.5 23.4 %collective-permute-start.3 = (f32[8,2,34,1]{3,0,2,1:T(8,128)S(1)}, f32[8,2,34,1]{3,0,2,1:T(8,128)S(1)}, u32[]{:S(2)}, u32[]{:S(2)}) collective-permute-start(f32[8,2,34,1]{3,0,2,1:T(8,128)S(1)} %get-tuple-element.26), channel_id=1, source_target_pairs={{0,1},{1,2},{2,3},{3,4},{4,5},{5,6},{6,7},{7,8},{8,9},{9,10},{10,1... | collective-permute-start | bytes 6536 | tf_op jit(solution)/shard_map/ppermute | solution.py:20
  18.9 36.0 %collective-permute-start.2 = (f32[8,2,34,1]{3,0,2,1:T(8,128)S(1)}, f32[8,2,34,1]{3,0,2,1:T(8,128)S(1)}, u32[]{:S(2)}, u32[]{:S(2)}) collective-permute-start(f32[8,2,34,1]{3,0,2,1:T(8,128)S(1)} %get-tuple-element.27), channel_id=1, source_target_pairs={{1,0},{2,1},{3,2},{4,3},{5,4},{6,5},{7,6},{8,7},{9,8},{10,9},{11,1... | collective-permute-start | bytes 6536 | tf_op jit(solution)/shard_map/ppermute | solution.py:22
  56.5 5.8 collective-permute-start.4
  60.4 5.3 collective-permute-start.5
  65.9 22.2 %collective-permute-start.7 = (f32[8,2,34,1]{3,0,2,1:T(8,128)S(1)}, f32[8,2,34,1]{3,0,2,1:T(8,128)S(1)}, u32[]{:S(2)}, u32[]{:S(2)}) collective-permute-start(f32[8,2,34,1]{3,0,2,1:T(8,128)S(1)} %get-tuple-element.24), channel_id=1, source_target_pairs={{0,1},{1,2},{2,3},{3,4},{4,5},{5,6},{6,7},{7,8},{8,9},{9,10},{10,1... | collective-permute-start | bytes 6536 | tf_op jit(solution)/shard_map/ppermute | solution.py:20
  67.8 23.3 %collective-permute-start.6 = (f32[8,2,34,1]{3,0,2,1:T(8,128)S(1)}, f32[8,2,34,1]{3,0,2,1:T(8,128)S(1)}, u32[]{:S(2)}, u32[]{:S(2)}) collective-permute-start(f32[8,2,34,1]{3,0,2,1:T(8,128)S(1)} %get-tuple-element.25), channel_id=1, source_target_pairs={{1,0},{2,1},{3,2},{4,3},{5,4},{6,5},{7,6},{8,7},{9,8},{10,9},{11,1... | collective-permute-start | bytes 6536 | tf_op jit(solution)/shard_map/ppermute | solution.py:22
  92.7 15.1 %collective-permute-start.8 = (f32[8,2,1,64]{3,0,2,1:T(8,128)S(1)}, f32[8,2,1,64]{3,0,2,1:T(8,128)S(1)}, u32[]{:S(2)}, u32[]{:S(2)}) collective-permute-start(f32[8,2,1,64]{3,0,2,1:T(8,128)S(1)} %get-tuple-element.49), channel_id=1, source_target_pairs={{16,0},{32,16},{48,32},{64,48},{80,64},{96,80},{112,96},{128,112},... | collective-permute-start | bytes 12296 | tf_op jit(solution)/shard_map/ppermute | solution.py:22
  105.8 5.0 collective-permute-start.9
  110.9 29.4 %collective-permute-start.11 = (f32[8,2,34,1]{3,0,2,1:T(8,128)S(1)}, f32[8,2,34,1]{3,0,2,1:T(8,128)S(1)}, u32[]{:S(2)}, u32[]{:S(2)}) collective-permute-start(f32[8,2,34,1]{3,0,2,1:T(8,128)S(1)} %get-tuple-element.22), channel_id=1, source_target_pairs={{0,1},{1,2},{2,3},{3,4},{4,5},{5,6},{6,7},{7,8},{8,9},{9,10},{10,1... | collective-permute-start | bytes 6536 | tf_op jit(solution)/shard_map/ppermute | solution.py:20
  112.9 27.4 %collective-permute-start.10 = (f32[8,2,34,1]{3,0,2,1:T(8,128)S(1)}, f32[8,2,34,1]{3,0,2,1:T(8,128)S(1)}, u32[]{:S(2)}, u32[]{:S(2)}) collective-permute-start(f32[8,2,34,1]{3,0,2,1:T(8,128)S(1)} %get-tuple-element.23), channel_id=1, source_target_pairs={{1,0},{2,1},{3,2},{4,3},{5,4},{6,5},{7,6},{8,7},{9,8},{10,9},{11,1... | collective-permute-start | bytes 6536 | tf_op jit(solution)/shard_map/ppermute | solution.py:22
  140.9 4.3 collective-permute-start.12
  142.8 5.0 collective-permute-start.13
  148.0 21.9 %collective-permute-start.14 = (f32[8,2,34,1]{3,0,2,1:T(8,128)S(1)}, f32[8,2,34,1]{3,0,2,1:T(8,128)S(1)}, u32[]{:S(2)}, u32[]{:S(2)}) collective-permute-start(f32[8,2,34,1]{3,0,2,1:T(8,128)S(1)} %get-tuple-element.21), channel_id=1, source_target_pairs={{1,0},{2,1},{3,2},{4,3},{5,4},{6,5},{7,6},{8,7},{9,8},{10,9},{11,1... | collective-permute-start | bytes 6536 | tf_op jit(solution)/shard_map/ppermute | solution.py:22
  158.2 27.7 %collective-permute-start.15 = (f32[8,2,34,1]{3,0,2,1:T(8,128)S(1)}, f32[8,2,34,1]{3,0,2,1:T(8,128)S(1)}, u32[]{:S(2)}, u32[]{:S(2)}) collective-permute-start(f32[8,2,34,1]{3,0,2,1:T(8,128)S(1)} %get-tuple-element.20), channel_id=1, source_target_pairs={{0,1},{1,2},{2,3},{3,4},{4,5},{5,6},{6,7},{7,8},{8,9},{9,10},{10,1... | collective-permute-start | bytes 6536 | tf_op jit(solution)/shard_map/ppermute | solution.py:20
  186.5 4.3 collective-permute-start.16
  188.4 5.0 collective-permute-start.17
  193.6 20.8 %collective-permute-start.19 = (f32[8,2,34,1]{3,0,2,1:T(8,128)S(1)}, f32[8,2,34,1]{3,0,2,1:T(8,128)S(1)}, u32[]{:S(2)}, u32[]{:S(2)}) collective-permute-start(f32[8,2,34,1]{3,0,2,1:T(8,128)S(1)} %get-tuple-element.18), channel_id=1, source_target_pairs={{0,1},{1,2},{2,3},{3,4},{4,5},{5,6},{6,7},{7,8},{8,9},{9,10},{10,1... | collective-permute-start | bytes 6536 | tf_op jit(solution)/shard_map/ppermute | solution.py:20
  195.5 18.8 %collective-permute-start.18 = (f32[8,2,34,1]{3,0,2,1:T(8,128)S(1)}, f32[8,2,34,1]{3,0,2,1:T(8,128)S(1)}, u32[]{:S(2)}, u32[]{:S(2)}) collective-permute-start(f32[8,2,34,1]{3,0,2,1:T(8,128)S(1)} %get-tuple-element.19), channel_id=1, source_target_pairs={{1,0},{2,1},{3,2},{4,3},{5,4},{6,5},{7,6},{8,7},{9,8},{10,9},{11,1... | collective-permute-start | bytes 6536 | tf_op jit(solution)/shard_map/ppermute | solution.py:22
  214.8 4.3 collective-permute-start.20
  216.7 5.0 collective-permute-start.21
  221.8 17.1 %collective-permute-start.23 = (f32[8,2,34,1]{3,0,2,1:T(8,128)S(1)}, f32[8,2,34,1]{3,0,2,1:T(8,128)S(1)}, u32[]{:S(2)}, u32[]{:S(2)}) collective-permute-start(f32[8,2,34,1]{3,0,2,1:T(8,128)S(1)} %get-tuple-element.16), channel_id=1, source_target_pairs={{0,1},{1,2},{2,3},{3,4},{4,5},{5,6},{6,7},{7,8},{8,9},{9,10},{10,1... | collective-permute-start | bytes 6536 | tf_op jit(solution)/shard_map/ppermute | solution.py:20
  223.8 16.3 %collective-permute-start.22 = (f32[8,2,34,1]{3,0,2,1:T(8,128)S(1)}, f32[8,2,34,1]{3,0,2,1:T(8,128)S(1)}, u32[]{:S(2)}, u32[]{:S(2)}) collective-permute-start(f32[8,2,34,1]{3,0,2,1:T(8,128)S(1)} %get-tuple-element.17), channel_id=1, source_target_pairs={{1,0},{2,1},{3,2},{4,3},{5,4},{6,5},{7,6},{8,7},{9,8},{10,9},{11,1... | collective-permute-start | bytes 6536 | tf_op jit(solution)/shard_map/ppermute | solution.py:22
  240.5 4.7 collective-permute-start.24
  243.3 5.8 collective-permute-start.25
  249.3 20.1 %collective-permute-start.27 = (f32[8,2,34,1]{3,0,2,1:T(8,128)S(1)}, f32[8,2,34,1]{3,0,2,1:T(8,128)S(1)}, u32[]{:S(2)}, u32[]{:S(2)}) collective-permute-start(f32[8,2,34,1]{3,0,2,1:T(8,128)S(1)} %get-tuple-element.14), channel_id=1, source_target_pairs={{0,1},{1,2},{2,3},{3,4},{4,5},{5,6},{6,7},{7,8},{8,9},{9,10},{10,1... | collective-permute-start | bytes 6536 | tf_op jit(solution)/shard_map/ppermute | solution.py:20
  251.2 18.2 %collective-permute-start.26 = (f32[8,2,34,1]{3,0,2,1:T(8,128)S(1)}, f32[8,2,34,1]{3,0,2,1:T(8,128)S(1)}, u32[]{:S(2)}, u32[]{:S(2)}) collective-permute-start(f32[8,2,34,1]{3,0,2,1:T(8,128)S(1)} %get-tuple-element.15), channel_id=1, source_target_pairs={{1,0},{2,1},{3,2},{4,3},{5,4},{6,5},{7,6},{8,7},{9,8},{10,9},{11,1... | collective-permute-start | bytes 6536 | tf_op jit(solution)/shard_map/ppermute | solution.py:22
  269.8 7.4 collective-permute-start.28
  275.3 5.2 collective-permute-start.29
  280.6 20.0 %collective-permute-start.30 = (f32[8,2,34,1]{3,0,2,1:T(8,128)S(1)}, f32[8,2,34,1]{3,0,2,1:T(8,128)S(1)}, u32[]{:S(2)}, u32[]{:S(2)}) collective-permute-start(f32[8,2,34,1]{3,0,2,1:T(8,128)S(1)} %get-tuple-element.13), channel_id=1, source_target_pairs={{1,0},{2,1},{3,2},{4,3},{5,4},{6,5},{7,6},{8,7},{9,8},{10,9},{11,1... | collective-permute-start | bytes 6536 | tf_op jit(solution)/shard_map/ppermute | solution.py:22
  287.8 18.1 %collective-permute-start.31 = (f32[8,2,34,1]{3,0,2,1:T(8,128)S(1)}, f32[8,2,34,1]{3,0,2,1:T(8,128)S(1)}, u32[]{:S(2)}, u32[]{:S(2)}) collective-permute-start(f32[8,2,34,1]{3,0,2,1:T(8,128)S(1)} %get-tuple-element.12), channel_id=1, source_target_pairs={{0,1},{1,2},{2,3},{3,4},{4,5},{5,6},{6,7},{7,8},{8,9},{9,10},{10,1... | collective-permute-start | bytes 6536 | tf_op jit(solution)/shard_map/ppermute | solution.py:20
  306.4 2.1 copy-start.3
  306.5 322.3 %copy-start.2 = (f32[8,2,32,64]{3,2,1,0:T(8,128)}, f32[8,2,32,64]{3,2,1,0:T(8,128)S(1)}, u32[]{:S(2)}) copy-start(f32[8,2,32,64]{3,2,1,0:T(8,128)S(1)} %copy.50) | copy-start | bytes 393220
  308.5 309.5 %all-gather.2.cloned.1.call-start = ((), (), s32[]{:S(2)}) async-start(), calls=%async_computation.4 | async-start | bytes 8650752 | tf_op jit(solution)/shard_map/all_gather | solution.py:65
  489.7 29.4 %all-to-all-start = ((f32[16,1,4096]{2,1,0:T(1,128)}), f32[16,1,4096]{2,1,0:T(1,128)S(1)}, u32[]{:S(2)}, u32[]{:S(2)}) async-start(f32[16,1,4096]{2,1,0:T(1,128)} %reshape.35), calls=%async_computation.1 | async-start | bytes 524288 | tf_op jit(solution)/shard_map/all_to_all | solution.py:78
  503.1 211.1 %reduce-scatter.9.cloned.1.call-start = ((), (), s32[]{:S(2)}) async-start(), calls=%async_computation.6 | async-start | bytes 540672 | tf_op jit(solution)/shard_map/reduce_scatter | solution.py:90
  524.3 307.9 %reduce-scatter.11.cloned.1.call-start = ((), (), s32[]{:S(2)}) async-start(), calls=%async_computation.7 | async-start | bytes 557056
Sparse Core Ops, SparseCore 0:
  308.6 179.2 reduce-scatter.6
  490.3 77.9 all-gather.1
  571.3 142.8 reduce-scatter.8
  718.1 113.9 reduce-scatter.10
